TPU v7x, 32 devices: a whole 2x2x4 slice. The times are simulated.
32 devices in a mesh: grp: 2 (over x), slab: 16 (over z, y, core).
Axes of the slice: x: 2, y: 2, z: 4, core: 2. Of those that a mesh axis runs over, the one named last changes fastest.
Arguments:
- states: float32 [1024, 128, 128], P(('grp', 'slab')), parts along dimension 0, may hold values from -30 to 30
- onsite_blocks: float32 [8, 128, 128], replicated, may hold values from -0.5 to 0.5
- hop_blocks: float32 [16, 128, 128], replicated, may hold values from -0.5 to 0.5
- onsite_index: int32 [1024], P(('grp', 'slab')), parts along dimension 0, may hold values from 0 to 7
- hop_index: int32 [1024, 4], P(('grp', 'slab')), parts along dimension 0, may hold values from 0 to 15, as said below
Outputs:
- basis: float32 [1024, 128, 128], P(('grp', 'slab')), parts along dimension 0
- reduced: float32 [256, 128], P('grp'), parts along dimension 0
There are 2 independent parts, one for each index of `grp`. A program takes and returns all parts, laid end to end along the dimension named above; an argument that names none is the same for every part. Nothing has to cross between parts.
Inputs may be any that keep to these rules, and one draw needn't show every extreme that they name: Consistent coupling: for every cell c, hop_index[c+1,1] = hop_index[c,2] and hop_index[c+2,0] = hop_index[c,3].
All inputs are finite; a program needn't handle non-finite values.
Results may differ from a plain program's by a relative error of at most 0.0001.
Values sent between devices are 32-bit elements; how exact they have to be, the bound alone decides.
A program may use at most 128 MiB of HBM per device.

v0:
```python
import functools

import jax
import jax.numpy as jnp
from jax import lax
from jax.experimental import pallas as pl
from jax.experimental.pallas import tpu as pltpu
from jax.sharding import PartitionSpec as P

DEGREE = 4
MESH = pl.DeviceIdType.MESH
BF = jnp.bfloat16
F32 = jnp.float32


def split2(x):
    hi = x.astype(BF)
    lo = (x - hi.astype(F32)).astype(BF)
    return hi, lo


def split3(x):
    hi = x.astype(BF).astype(F32)
    rest = x - hi
    mid = rest.astype(BF).astype(F32)
    return hi, mid, rest - mid


def kernel(
    n,
    owners,
    hop_idx,
    on_idx,
    states,
    onsite,
    hop,
    f4,
    inv_out,
    red_out,
    sym_t,
    half_t,
    hop_t,
    hopt_t,
    wa,
    wb,
    fa,
    fb,
    wt,
    halo_l,
    halo_r,
    gacc,
    part,
    inbox,
    share,
    full,
    aug,
    halo_send,
    halo_recv,
    rs_send,
    rs_recv,
    ag_send,
    ag_recv,
):
    me = lax.axis_index("slab")
    cells, orb, width = states.shape
    stride = n // owners
    rows = width // owners
    non = onsite.shape[0]
    nhop = hop.shape[0]

    barrier = pltpu.get_barrier_semaphore()

    @pl.loop(1, n)
    def _(d):
        pl.semaphore_signal(
            barrier, inc=1, device_id={"slab": lax.rem(me + d, n)}, device_id_type=MESH
        )

    def put(w, at, x):
        hi, lo = split2(x)
        w[at, :, 0:width] = hi
        w[at, :, width : 2 * width] = lo

    def table(ref, at, x):
        hi, lo = split2(x)
        ref[at, 0:orb, :] = hi
        ref[at, orb : 2 * orb, :] = lo

    zero2 = jnp.zeros((2, orb, 2 * width), BF)
    for w in (wa, wb):
        w[0:2] = zero2
        w[cells + 2 : cells + 4] = zero2

    pl.semaphore_wait(barrier, n - 1)

    def halo(k, src):
        left = pltpu.make_async_remote_copy(
            src_ref=src.at[0:2],
            dst_ref=halo_r.at[k],
            send_sem=halo_send.at[k, 0],
            recv_sem=halo_recv.at[k, 0],
            device_id={"slab": jnp.maximum(me - 1, 0)},
            device_id_type=MESH,
        )
        right = pltpu.make_async_remote_copy(
            src_ref=src.at[cells - 2 : cells],
            dst_ref=halo_l.at[k],
            send_sem=halo_send.at[k, 1],
            recv_sem=halo_recv.at[k, 1],
            device_id={"slab": jnp.minimum(me + 1, n - 1)},
            device_id_type=MESH,
        )
        return left, right

    def halo_start(k, src):
        left, right = halo(k, src)
        pl.when(me > 0)(left.start)
        if k < DEGREE:
            pl.when(me < n - 1)(right.start)

    def halo_wait(k, src, w):
        left, right = halo(k, src)

        @pl.when(me > 0)
        def _():
            left.wait_send()
            if k < DEGREE:
                right.wait_recv()
                for i in range(2):
                    put(w, i, halo_l[k, i])

        @pl.when(me < n - 1)
        def _():
            if k < DEGREE:
                right.wait_send()
            left.wait_recv()
            for i in range(2):
                put(w, cells + 2 + i, halo_r[k, i])

    halo_start(0, states)

    @pl.loop(0, non)
    def _(i):
        block = onsite[i]
        sym = 0.5 * (block + block.T)
        table(sym_t, i, sym)
        table(half_t, i, 0.5 * sym)

    @pl.loop(0, nhop)
    def _(i):
        block = hop[i]
        table(hop_t, i, block)
        table(hopt_t, i, block.T)

    @pl.loop(0, cells)
    def _(c):
        put(wa, c + 2, states[c])

    halo_wait(0, states, wa)

    def fold(acc):
        return acc[:orb, :width] + (acc[:orb, width:] + acc[orb:, :width])

    def apply_cell(w, c):
        lhs = jnp.concatenate(
            [
                hopt_t[hop_idx[c, 0]],
                hopt_t[hop_idx[c, 1]],
                sym_t[on_idx[c]],
                hop_t[hop_idx[c, 2]],
                hop_t[hop_idx[c, 3]],
            ],
            axis=1,
        )
        rhs = w[pl.ds(c, 5)].reshape(5 * orb, 2 * width)
        return fold(jnp.dot(lhs, rhs, preferred_element_type=F32))

    def step(k, w, w_next, cur, prev, out):
        def one(c):
            image = apply_cell(w, c)
            if k == 0:
                new = (image - 1.5 * cur[c]) * (1.0 / 3.0)
            else:
                new = (image - 1.5 * cur[c]) * (2.0 / 3.0) - prev[c]
            out[c] = new
            put(w_next, c + 2, new)
            if k == DEGREE - 1:
                hi, lo = split2(new.T)
                wt[c, 0:width, :] = hi
                wt[c, width : 2 * width, :] = lo

        for c in (0, 1, cells - 2, cells - 1):
            one(c)
        halo_start(k + 1, out)

        @pl.loop(2, cells - 2, step=4)
        def _(c):
            for i in range(4):
                one(c + i)

    step(0, wa, wb, states, None, fa)
    halo_wait(1, fa, wb)
    step(1, wb, wa, fa, states, fb)
    halo_wait(2, fb, wa)
    step(2, wa, wb, fb, fa, fa)
    halo_wait(3, fa, wb)
    step(3, wb, wa, fa, fb, f4)

    def rs_copy(s, t):
        return pltpu.make_async_remote_copy(
            src_ref=part.at[s, pl.ds(t * rows, rows)],
            dst_ref=inbox.at[s, me],
            send_sem=rs_send.at[s, t],
            recv_sem=rs_recv.at[s, me],
            device_id={"slab": t * stride},
            device_id_type=MESH,
        )

    def rs_start(s):
        @pl.loop(0, owners)
        def _(t):
            @pl.when(t * stride != me)
            def _():
                rs_copy(s, t).start()

    mine = me // stride

    def ag_copy(s, d):
        return pltpu.make_async_remote_copy(
            src_ref=share.at[s],
            dst_ref=full.at[s, pl.ds(mine * rows, rows)],
            send_sem=ag_send.at[s, d],
            recv_sem=ag_recv.at[s, mine],
            device_id={"slab": lax.rem(me + d, n)},
            device_id_type=MESH,
        )

    def owner(f):
        if stride == 1:
            f()
        else:
            pl.when(me == mine * stride)(f)

    def rs_finish(s):
        @pl.loop(0, owners)
        def _(t):
            @pl.when(t * stride != me)
            def _():
                rs_copy(s, t).wait_send()

        @owner
        def _():
            share[s] = part[s, pl.ds(mine * rows, rows)]

            @pl.loop(1, n)
            def _(d):
                src = lax.rem(me + d, n)
                pltpu.make_async_remote_copy(
                    src_ref=inbox.at[s, src],
                    dst_ref=inbox.at[s, src],
                    send_sem=rs_send.at[s, 0],
                    recv_sem=rs_recv.at[s, src],
                    device_id={"slab": src},
                    device_id_type=MESH,
                ).wait_recv()
                share[s] = share[s] + inbox[s, src]

            @pl.loop(1, n)
            def _(d):
                ag_copy(s, d).start()

            full[s, pl.ds(mine * rows, rows)] = share[s]

    def ag_finish(s):
        @owner
        def _():
            @pl.loop(1, n)
            def _(d):
                ag_copy(s, d).wait_send()

        @pl.loop(0, owners)
        def _(t):
            @pl.when(t * stride != me)
            def _():
                pltpu.make_async_remote_copy(
                    src_ref=share.at[s],
                    dst_ref=full.at[s, pl.ds(t * rows, rows)],
                    send_sem=ag_send.at[s, 0],
                    recv_sem=ag_recv.at[s, t],
                    device_id={"slab": t * stride},
                    device_id_type=MESH,
                ).wait_recv()

    gacc[...] = jnp.zeros_like(gacc)

    @pl.loop(0, cells, step=4)
    def _(c):
        lhs = jnp.concatenate([wt[c + i] for i in range(4)], axis=1)
        rhs = wa[pl.ds(c + 2, 4)].reshape(4 * orb, 2 * width)
        gacc[...] += jnp.dot(lhs, rhs, preferred_element_type=F32)

    part[0] = fold(gacc)
    rs_start(0)

    gacc[...] = jnp.zeros_like(gacc)

    def half_image(c):
        lhs = jnp.concatenate(
            [half_t[on_idx[c]], hop_t[hop_idx[c, 2]], hop_t[hop_idx[c, 3]]], axis=1
        )
        rhs = wa[pl.ds(c + 2, 3)].reshape(3 * orb, 2 * width)
        return fold(jnp.dot(lhs, rhs, preferred_element_type=F32))

    def project(c):
        images = []
        for i in range(4):
            hi, lo = split2(half_image(c + i))
            images.append(jnp.concatenate([hi, lo], axis=1))
        lhs = jnp.concatenate([wt[c + i] for i in range(4)], axis=1)
        gacc[...] += jnp.dot(
            lhs, jnp.concatenate(images, axis=0), preferred_element_type=F32
        )

    middle = cells // 2

    @pl.loop(0, middle, step=4)
    def _(c):
        project(c)

    rs_finish(0)
    halo_wait(4, f4, wa)

    @pl.loop(middle, cells, step=4)
    def _(c):
        project(c)

    part[1] = fold(gacc)
    rs_start(1)

    ag_finish(0)
    aug[:, 0:width] = full[0]
    row = lax.broadcasted_iota(jnp.int32, (width, width), 0)
    col = lax.broadcasted_iota(jnp.int32, (width, width), 1)
    aug[:, width : 2 * width] = jnp.where(row == col, 1.0, 0.0).astype(F32)

    def chol_block(b):
        base = 8 * b
        panel = aug[base : base + 8, :]
        s = {}
        for i in range(8):
            for k in range(i, 8):
                s[i, k] = jnp.broadcast_to(
                    panel[i : i + 1, base + k : base + k + 1], (1, 2 * width)
                )
        lines = [panel[i : i + 1, :] for i in range(8)]
        done = []
        for i in range(8):
            inv = lax.rsqrt(s[i, i])
            line = lines[i] * inv
            done.append(line)
            low = {k: s[i, k] * inv for k in range(i + 1, 8)}
            for k in range(i + 1, 8):
                lines[k] = lines[k] - low[k] * line
                for m in range(k, 8):
                    s[k, m] = s[k, m] - low[k] * low[m]
        upper = jnp.concatenate(done, axis=0)
        aug[base : base + 8, :] = upper
        if base + 8 < width:
            hi, mid, lo = split3(upper)
            left = jnp.concatenate([hi, hi, mid, hi, mid, lo], axis=0)[:, 0:width]
            right = jnp.concatenate([hi, mid, hi, lo, mid, hi], axis=0)
            update = lax.dot_general(
                left.T.astype(BF),
                right.astype(BF),
                (((1,), (0,)), ((), ())),
                preferred_element_type=F32,
            )
            aug[base + 8 :, :] = aug[base + 8 :, :] - update[base + 8 :, :]

    blocks = width // 8
    for b in range(blocks // 2):
        chol_block(b)
    rs_finish(1)
    for b in range(blocks // 2, blocks):
        chol_block(b)
    ag_finish(1)

    inverse = aug[:, width : 2 * width]
    inv_out[...] = inverse
    upper = full[1]
    projected = upper + upper.T
    highest = lax.Precision.HIGHEST
    right = jnp.dot(inverse, projected, precision=highest, preferred_element_type=F32)
    red_out[...] = lax.dot_general(
        right,
        inverse,
        (((1,), (1,)), ((), ())),
        precision=highest,
        preferred_element_type=F32,
    )


def local(states, onsite_blocks, hop_blocks, onsite_index, hop_index):
    cells, orb, width = states.shape
    n = lax.axis_size("slab")
    owners = min(n, width // 8)
    rows = width // owners
    non, nhop = onsite_blocks.shape[0], hop_blocks.shape[0]
    vmem = pl.BlockSpec(memory_space=pltpu.VMEM)
    smem = pl.BlockSpec(memory_space=pltpu.SMEM)
    field = pltpu.VMEM((cells, orb, width), F32)
    wide = pltpu.VMEM((cells + 4, orb, 2 * width), BF)
    halo = pltpu.VMEM((DEGREE + 1, 2, orb, width), F32)
    dma = pltpu.SemaphoreType.DMA
    current, inverse, reduced = pl.pallas_call(
        functools.partial(kernel, n, owners),
        out_shape=(
            jax.ShapeDtypeStruct((cells, orb, width), F32),
            jax.ShapeDtypeStruct((width, width), F32),
            jax.ShapeDtypeStruct((width, width), F32),
        ),
        in_specs=[smem, smem, vmem, vmem, vmem],
        out_specs=(vmem, vmem, vmem),
        scratch_shapes=[
            pltpu.VMEM((non, 2 * orb, orb), BF),
            pltpu.VMEM((non, 2 * orb, orb), BF),
            pltpu.VMEM((nhop, 2 * orb, orb), BF),
            pltpu.VMEM((nhop, 2 * orb, orb), BF),
            wide,
            wide,
            field,
            field,
            pltpu.VMEM((cells, 2 * width, orb), BF),
            halo,
            halo,
            pltpu.VMEM((2 * width, 2 * width), F32),
            pltpu.VMEM((2, width, width), F32),
            pltpu.VMEM((2, n, rows, width), F32),
            pltpu.VMEM((2, rows, width), F32),
            pltpu.VMEM((2, width, width), F32),
            pltpu.VMEM((width, 2 * width), F32),
            dma((DEGREE + 1, 2)),
            dma((DEGREE + 1, 2)),
            dma((2, owners)),
            dma((2, n)),
            dma((2, n)),
            dma((2, owners)),
        ],
        compiler_params=pltpu.CompilerParams(
            collective_id=0, has_side_effects=True, vmem_limit_bytes=50 * 2**20
        ),
        name="filter",
    )(hop_index, onsite_index, states, onsite_blocks, hop_blocks)
    total = cells * n
    factor = jnp.sqrt(jnp.float32(total * orb))
    basis = jnp.einsum(
        "cis,ts->cit", current, inverse * factor, precision=lax.Precision.HIGH
    )
    return (basis, reduced)


def solution(mesh):
    placed = (
        P(("grp", "slab"), None, None),
        P(),
        P(),
        P(("grp", "slab")),
        P(("grp", "slab"), None),
    )
    return jax.shard_map(
        local,
        mesh=mesh,
        in_specs=placed,
        out_specs=(P(("grp", "slab"), None, None), P("grp", None)),
        check_vma=False,
    )
```

profile of v0, /device:TPU:0, one launch (start us, length us, event | category | flops | bytes accessed | tf_op | source)
XLA Modules:
  0.0 58.4 jit_solution(2032240672016821918)
XLA Ops:
  0.6 0.8 %copy.7.hop_idx = s32[32,4]{1,0:T(8,128)S(1)} copy(s32[32,4]{0,1:T(4,128)} %param.9) | data formatting | bytes 1024 | tf_op args[4]
  1.4 0.0 copy-start
  1.4 1.2 %copy-done = f32[16,128,128]{2,1,0:T(8,128)S(1)} copy-done((f32[16,128,128]{2,1,0:T(8,128)S(1)}, f32[16,128,128]{2,1,0:T(8,128)}, u32[]{:S(2)}) %copy-start) | copy-done | bytes 1048600
  2.6 0.0 copy-start.1
  2.6 1.0 %copy-done.1 = f32[8,128,128]{2,1,0:T(8,128)S(1)} copy-done((f32[8,128,128]{2,1,0:T(8,128)S(1)}, f32[8,128,128]{2,1,0:T(8,128)}, u32[]{:S(2)}) %copy-start.1) | copy-done | bytes 524312
  3.7 0.0 copy-start.2
  3.7 0.7 %copy-done.2 = s32[32]{0:T(128)S(1)} copy-done((s32[32]{0:T(128)S(1)}, s32[32]{0:T(128)}, u32[]{:S(2)}) %copy-start.2) | copy-done | bytes 152
  4.3 51.1 %filter.1 = (f32[32,128,128]{2,1,0:T(8,128)S(1)}, f32[128,128]{1,0:T(8,128)S(1)}, f32[128,128]{1,0:T(8,128)S(1)}) custom-call(s32[32,4]{1,0:T(8,128)S(1)} %copy.7.hop_idx, s32[32]{0:T(128)S(1)} %copy-done.2, f32[32,128,128]{2,1,0:T(8,128)} %states.1, f32[8,128,128]{2,1,0:T(8,128)S(1)} %copy-done.1, f32[16,128,128]{2,1,0:T(8,128)S(1)} %copy-done), custom_call_target="tpu_custom_call" | custom-call | tf_op jit(solution)/shard_map/filter/pallas_call | solution.py:415
  55.4 2.3 %fusion = f32[32,128,128]{2,1,0:T(8,128)} fusion(f32[32,128,128]{2,1,0:T(8,128)S(1)} %get-tuple-element.5, f32[128,128]{1,0:T(8,128)S(1)} %get-tuple-element.6), kind=kOutput, calls=%fused_computation | convolution fusion | flops 402669568 | bytes 4259840 | tf_op jit(solution)/shard_map/cis,ts->cit/dot_general | solution.py:456
  57.8 0.6 %copy.9 = f32[128,128]{1,0:T(8,128)} copy(f32[128,128]{1,0:T(8,128)S(1)} %get-tuple-element.11) | data formatting | bytes 131072
Async XLA Ops:
  1.4 1.2 %copy-start = (f32[16,128,128]{2,1,0:T(8,128)S(1)}, f32[16,128,128]{2,1,0:T(8,128)}, u32[]{:S(2)}) copy-start(f32[16,128,128]{2,1,0:T(8,128)} %hop.1) | copy-start | bytes 3145732
  2.6 1.0 %copy-start.1 = (f32[8,128,128]{2,1,0:T(8,128)S(1)}, f32[8,128,128]{2,1,0:T(8,128)}, u32[]{:S(2)}) copy-start(f32[8,128,128]{2,1,0:T(8,128)} %onsite.1) | copy-start | bytes 1572868
  3.7 0.7 %copy-start.2 = (s32[32]{0:T(128)S(1)}, s32[32]{0:T(128)}, u32[]{:S(2)}) copy-start(s32[32]{0:T(128)} %on_idx.1) | copy-start | bytes 388
where the time goes:
time: 58.7 us; the launch traced here: 58.4 us
  Pallas kernels  51.1 us (87%)
  local copies, waits for them, and re-layouts  4.31 us (7%)
  matrix products  2.32 us (4%)
  between operations  0.64 us (1%)
    pallas_call x1, Pallas kernels, local(): pl.pallas_call(functools.partial(kernel, n, owners), out_shape=(jax.Shape...  51.1 us
    unnamed x8, local copies, waits for them, and re-layouts  4.31 us
    dot_general x1, matrix products, local(): jnp.einsum('cis,ts->cit', current, inverse * factor, precision=lax.Precis...  2.32 us

commit v1 on v0

--- a/solution.py
+++ b/solution.py
@@ -31,12 +31,15 @@
     owners,
     hop_idx,
     on_idx,
+    states_hbm,
+    onsite_hbm,
+    hop_hbm,
+    wide_out,
+    inv_out,
+    proj_out,
     states,
     onsite,
     hop,
-    f4,
-    inv_out,
-    red_out,
     sym_t,
     half_t,
     hop_t,
@@ -60,6 +63,8 @@
     rs_recv,
     ag_send,
     ag_recv,
+    load_sem,
+    store_sem,
 ):
     me = lax.axis_index("slab")
     cells, orb, width = states.shape
@@ -76,6 +81,15 @@
             barrier, inc=1, device_id={"slab": lax.rem(me + d, n)}, device_id_type=MESH
         )
 
+    loads = [
+        pltpu.make_async_copy(src, dst, load_sem.at[i])
+        for i, (src, dst) in enumerate(
+            ((hop_hbm, hop), (onsite_hbm, onsite), (states_hbm, states))
+        )
+    ]
+    for load in loads:
+        load.start()
+
     def put(w, at, x):
         hi, lo = split2(x)
         w[at, :, 0:width] = hi
@@ -83,8 +97,8 @@
 
     def table(ref, at, x):
         hi, lo = split2(x)
-        ref[at, 0:orb, :] = hi
-        ref[at, orb : 2 * orb, :] = lo
+        ref[at, :, 0:orb] = hi
+        ref[at, :, orb : 2 * orb] = lo
 
     zero2 = jnp.zeros((2, orb, 2 * width), BF)
     for w in (wa, wb):
@@ -137,43 +151,54 @@
             for i in range(2):
                 put(w, cells + 2 + i, halo_r[k, i])
 
-    halo_start(0, states)
-
-    @pl.loop(0, non)
+    halo_start(0, states_hbm)
+
+    loads[0].wait()
+    loads[1].wait()
+
+    @pl.loop(0, non, unroll=True)
     def _(i):
         block = onsite[i]
         sym = 0.5 * (block + block.T)
         table(sym_t, i, sym)
         table(half_t, i, 0.5 * sym)
 
-    @pl.loop(0, nhop)
+    @pl.loop(0, nhop, unroll=4)
     def _(i):
         block = hop[i]
         table(hop_t, i, block)
         table(hopt_t, i, block.T)
 
-    @pl.loop(0, cells)
+    loads[2].wait()
+
+    @pl.loop(0, cells, unroll=4)
     def _(c):
         put(wa, c + 2, states[c])
 
-    halo_wait(0, states, wa)
+    halo_wait(0, states_hbm, wa)
 
     def fold(acc):
-        return acc[:orb, :width] + (acc[:orb, width:] + acc[orb:, :width])
+        return acc[:, :width] + acc[:, width:]
+
+    def twice(w, at, count):
+        parts = []
+        for i in range(count):
+            block = w[at + i]
+            parts += [block, block]
+        return jnp.concatenate(parts, axis=0)
 
     def apply_cell(w, c):
         lhs = jnp.concatenate(
             [
-                hopt_t[hop_idx[c, 0]],
-                hopt_t[hop_idx[c, 1]],
+                hopt_t[hop_idx[0, c]],
+                hopt_t[hop_idx[1, c]],
                 sym_t[on_idx[c]],
-                hop_t[hop_idx[c, 2]],
-                hop_t[hop_idx[c, 3]],
+                hop_t[hop_idx[2, c]],
+                hop_t[hop_idx[3, c]],
             ],
             axis=1,
         )
-        rhs = w[pl.ds(c, 5)].reshape(5 * orb, 2 * width)
-        return fold(jnp.dot(lhs, rhs, preferred_element_type=F32))
+        return fold(jnp.dot(lhs, twice(w, c, 5), preferred_element_type=F32))
 
     def step(k, w, w_next, cur, prev, out):
         def one(c):
@@ -186,16 +211,19 @@
             put(w_next, c + 2, new)
             if k == DEGREE - 1:
                 hi, lo = split2(new.T)
-                wt[c, 0:width, :] = hi
-                wt[c, width : 2 * width, :] = lo
+                wt[c, :, 0:orb] = hi
+                wt[c, :, orb : 2 * orb] = lo
 
         for c in (0, 1, cells - 2, cells - 1):
             one(c)
         halo_start(k + 1, out)
 
-        @pl.loop(2, cells - 2, step=4)
+        inner = cells - 4
+        group = max(d for d in range(1, 15) if inner % d == 0)
+
+        @pl.loop(2, cells - 2, step=group)
         def _(c):
-            for i in range(4):
+            for i in range(group):
                 one(c + i)
 
     step(0, wa, wb, states, None, fa)
@@ -204,7 +232,11 @@
     halo_wait(2, fb, wa)
     step(2, wa, wb, fb, fa, fa)
     halo_wait(3, fa, wb)
-    step(3, wb, wa, fa, fb, f4)
+    step(3, wb, wa, fa, fb, fb)
+    store = pltpu.make_async_copy(
+        wa.at[2 : cells + 2], wide_out, store_sem
+    )
+    store.start()
 
     def rs_copy(s, t):
         return pltpu.make_async_remote_copy(
@@ -291,13 +323,15 @@
                     device_id_type=MESH,
                 ).wait_recv()
 
+    batch = max(d for d in range(1, 9) if cells % (2 * d) == 0)
     gacc[...] = jnp.zeros_like(gacc)
 
-    @pl.loop(0, cells, step=4)
+    @pl.loop(0, cells, step=batch)
     def _(c):
-        lhs = jnp.concatenate([wt[c + i] for i in range(4)], axis=1)
-        rhs = wa[pl.ds(c + 2, 4)].reshape(4 * orb, 2 * width)
-        gacc[...] += jnp.dot(lhs, rhs, preferred_element_type=F32)
+        lhs = jnp.concatenate([wt[c + i] for i in range(batch)], axis=1)
+        gacc[...] += jnp.dot(
+            lhs, twice(wa, c + 2, batch), preferred_element_type=F32
+        )
 
     part[0] = fold(gacc)
     rs_start(0)
@@ -306,31 +340,31 @@
 
     def half_image(c):
         lhs = jnp.concatenate(
-            [half_t[on_idx[c]], hop_t[hop_idx[c, 2]], hop_t[hop_idx[c, 3]]], axis=1
-        )
-        rhs = wa[pl.ds(c + 2, 3)].reshape(3 * orb, 2 * width)
-        return fold(jnp.dot(lhs, rhs, preferred_element_type=F32))
+            [half_t[on_idx[c]], hop_t[hop_idx[2, c]], hop_t[hop_idx[3, c]]], axis=1
+        )
+        return fold(jnp.dot(lhs, twice(wa, c + 2, 3), preferred_element_type=F32))
 
     def project(c):
         images = []
-        for i in range(4):
+        for i in range(batch):
             hi, lo = split2(half_image(c + i))
-            images.append(jnp.concatenate([hi, lo], axis=1))
-        lhs = jnp.concatenate([wt[c + i] for i in range(4)], axis=1)
+            both = jnp.concatenate([hi, lo], axis=1)
+            images += [both, both]
+        lhs = jnp.concatenate([wt[c + i] for i in range(batch)], axis=1)
         gacc[...] += jnp.dot(
             lhs, jnp.concatenate(images, axis=0), preferred_element_type=F32
         )
 
     middle = cells // 2
 
-    @pl.loop(0, middle, step=4)
+    @pl.loop(0, middle, step=batch)
     def _(c):
         project(c)
 
     rs_finish(0)
-    halo_wait(4, f4, wa)
-
-    @pl.loop(middle, cells, step=4)
+    halo_wait(4, fb, wa)
+
+    @pl.loop(middle, cells, step=batch)
     def _(c):
         project(c)
 
@@ -385,19 +419,44 @@
         chol_block(b)
     ag_finish(1)
 
-    inverse = aug[:, width : 2 * width]
-    inv_out[...] = inverse
+    inv_out[...] = aug[:, width : 2 * width]
     upper = full[1]
-    projected = upper + upper.T
-    highest = lax.Precision.HIGHEST
-    right = jnp.dot(inverse, projected, precision=highest, preferred_element_type=F32)
-    red_out[...] = lax.dot_general(
-        right,
-        inverse,
-        (((1,), (1,)), ((), ())),
-        precision=highest,
+    proj_out[...] = upper + upper.T
+    store.wait()
+
+
+def finish(factor, wide, inv, proj, basis, reduced, weights):
+    count, orb, double = wide.shape
+    width = double // 2
+    inverse = inv[...]
+
+    @pl.when(pl.program_id(0) == 0)
+    def _():
+        hi, lo = split2(inverse.T * factor)
+        for i in range(2):
+            weights[i * width : (i + 1) * width, 0:width] = hi
+            weights[i * width : (i + 1) * width, width : 2 * width] = lo
+
+    both = jnp.dot(
+        wide[...].reshape(count * orb, double),
+        weights[...],
         preferred_element_type=F32,
     )
+    basis[...] = (both[:, :width] + both[:, width:]).reshape(count, orb, width)
+
+    @pl.when(pl.program_id(0) == 0)
+    def _():
+        highest = lax.Precision.HIGHEST
+        right = jnp.dot(
+            inverse, proj[...], precision=highest, preferred_element_type=F32
+        )
+        reduced[...] = lax.dot_general(
+            right,
+            inverse,
+            (((1,), (1,)), ((), ())),
+            precision=highest,
+            preferred_element_type=F32,
+        )
 
 
 def local(states, onsite_blocks, hop_blocks, onsite_index, hop_index):
@@ -407,33 +466,37 @@
     rows = width // owners
     non, nhop = onsite_blocks.shape[0], hop_blocks.shape[0]
     vmem = pl.BlockSpec(memory_space=pltpu.VMEM)
+    hbm = pl.BlockSpec(memory_space=pl.ANY)
     smem = pl.BlockSpec(memory_space=pltpu.SMEM)
     field = pltpu.VMEM((cells, orb, width), F32)
     wide = pltpu.VMEM((cells + 4, orb, 2 * width), BF)
     halo = pltpu.VMEM((DEGREE + 1, 2, orb, width), F32)
     dma = pltpu.SemaphoreType.DMA
-    current, inverse, reduced = pl.pallas_call(
+    current, inverse, projected = pl.pallas_call(
         functools.partial(kernel, n, owners),
         out_shape=(
-            jax.ShapeDtypeStruct((cells, orb, width), F32),
+            jax.ShapeDtypeStruct((cells, orb, 2 * width), BF),
             jax.ShapeDtypeStruct((width, width), F32),
             jax.ShapeDtypeStruct((width, width), F32),
         ),
-        in_specs=[smem, smem, vmem, vmem, vmem],
-        out_specs=(vmem, vmem, vmem),
+        in_specs=[smem, smem, hbm, hbm, hbm],
+        out_specs=(hbm, vmem, vmem),
         scratch_shapes=[
-            pltpu.VMEM((non, 2 * orb, orb), BF),
-            pltpu.VMEM((non, 2 * orb, orb), BF),
-            pltpu.VMEM((nhop, 2 * orb, orb), BF),
-            pltpu.VMEM((nhop, 2 * orb, orb), BF),
+            field,
+            pltpu.VMEM((non, orb, orb), F32),
+            pltpu.VMEM((nhop, orb, orb), F32),
+            pltpu.VMEM((non, orb, 2 * orb), BF),
+            pltpu.VMEM((non, orb, 2 * orb), BF),
+            pltpu.VMEM((nhop, orb, 2 * orb), BF),
+            pltpu.VMEM((nhop, orb, 2 * orb), BF),
             wide,
             wide,
             field,
             field,
-            pltpu.VMEM((cells, 2 * width, orb), BF),
+            pltpu.VMEM((cells, width, 2 * orb), BF),
             halo,
             halo,
-            pltpu.VMEM((2 * width, 2 * width), F32),
+            pltpu.VMEM((width, 2 * width), F32),
             pltpu.VMEM((2, width, width), F32),
             pltpu.VMEM((2, n, rows, width), F32),
             pltpu.VMEM((2, rows, width), F32),
@@ -445,17 +508,35 @@
             dma((2, n)),
             dma((2, n)),
             dma((2, owners)),
+            dma((3,)),
+            dma,
         ],
         compiler_params=pltpu.CompilerParams(
-            collective_id=0, has_side_effects=True, vmem_limit_bytes=50 * 2**20
+            collective_id=0, has_side_effects=True, vmem_limit_bytes=60 * 2**20
         ),
         name="filter",
-    )(hop_index, onsite_index, states, onsite_blocks, hop_blocks)
+    )(hop_index.T, onsite_index, states, onsite_blocks, hop_blocks)
     total = cells * n
-    factor = jnp.sqrt(jnp.float32(total * orb))
-    basis = jnp.einsum(
-        "cis,ts->cit", current, inverse * factor, precision=lax.Precision.HIGH
-    )
+    factor = float(total * orb) ** 0.5
+    count = max(d for d in range(1, 9) if cells % d == 0)
+    square = pl.BlockSpec((width, width), lambda i: (0, 0))
+    basis, reduced = pl.pallas_call(
+        functools.partial(finish, factor),
+        grid=(cells // count,),
+        out_shape=(
+            jax.ShapeDtypeStruct((cells, orb, width), F32),
+            jax.ShapeDtypeStruct((width, width), F32),
+        ),
+        in_specs=[
+            pl.BlockSpec((count, orb, 2 * width), lambda i: (i, 0, 0)),
+            square,
+            square,
+        ],
+        out_specs=(pl.BlockSpec((count, orb, width), lambda i: (i, 0, 0)), square),
+        scratch_shapes=[pltpu.VMEM((2 * width, 2 * width), BF)],
+        compiler_params=pltpu.CompilerParams(vmem_limit_bytes=32 * 2**20),
+        name="finish",
+    )(current, inverse, projected)
     return (basis, reduced)
 
 

time: 58.7 us -> 54.8 us (0.934)
  matrix products: 2.32 us -> 0 us
  local copies, waits for them, and re-layouts: 4.31 us -> 3.26 us
    pallas_call x1, Pallas kernels: 51.1 us -> 47.5 us  [local(): pl.pallas_call(functools.partial(kernel, n, owners), out_shape=(jax.Shape...]
    pallas_call x0 -> x1, Pallas kernels: none -> 3.12 us  [local(): pl.pallas_call(functools.partial(finish, factor), grid=(cells // count,),...]
    dot_general x1 -> x0, matrix products: 2.32 us -> none  [local(): jnp.einsum('cis,ts->cit', current, inverse * factor, precision=lax.Precis...]
    unnamed x8 -> x6, local copies, waits for them, and re-layouts: 4.31 us -> 3.26 us
where the time goes in v1:
time: 54.8 us; the launch traced here: 54.5 us
  Pallas kernels  50.6 us (92%)
  local copies, waits for them, and re-layouts  3.26 us (6%)
  between operations  0.65 us (1%)
    pallas_call x1, Pallas kernels, local(): pl.pallas_call(functools.partial(kernel, n, owners), out_shape=(jax.Shape...  47.5 us
    unnamed x6, local copies, waits for them, and re-layouts  3.26 us
    pallas_call x1, Pallas kernels, local(): pl.pallas_call(functools.partial(finish, factor), grid=(cells // count,),...  3.12 us

profile of v1, /device:TPU:0, one launch (start us, length us, event | category | flops | bytes accessed | tf_op | source)
XLA Modules:
  0.0 54.5 jit_solution(1539221826316189652)
XLA Ops:
  0.6 47.5 %filter.1 = (bf16[32,128,256]{2,1,0:T(8,128)(2,1)}, f32[128,128]{1,0:T(8,128)}, f32[128,128]{1,0:T(8,128)}) custom-call(s32[4,32]{1,0:T(4,128)} %bitcast.1, s32[32]{0:T(128)} %on_idx.1, f32[32,128,128]{2,1,0:T(8,128)} %states_hbm.1, f32[8,128,128]{2,1,0:T(8,128)} %onsite_hbm.1, f32[16,128,128]{2,1,0:T(8,128)} %hop_hbm.1), custom_call_target="tpu_custom_call" | custom-call | tf_op jit(solution)/shard_map/filter/pallas_call | solution.py:475
  48.2 0.0 copy-start
  48.2 1.6 %copy-done = bf16[32,128,256]{2,1,0:T(8,128)(2,1)S(1)} copy-done((bf16[32,128,256]{2,1,0:T(8,128)(2,1)S(1)}, bf16[32,128,256]{2,1,0:T(8,128)(2,1)}, u32[]{:S(2)}) %copy-start) | copy-done | bytes 2097176
  49.7 0.0 copy-start.1
  49.7 0.8 %copy-done.1 = f32[128,128]{1,0:T(8,128)S(1)} copy-done((f32[128,128]{1,0:T(8,128)S(1)}, f32[128,128]{1,0:T(8,128)}, u32[]{:S(2)}) %copy-start.1) | copy-done | bytes 65560
  50.6 0.0 copy-start.2
  50.6 0.8 %copy-done.2 = f32[128,128]{1,0:T(8,128)S(1)} copy-done((f32[128,128]{1,0:T(8,128)S(1)}, f32[128,128]{1,0:T(8,128)}, u32[]{:S(2)}) %copy-start.2) | copy-done | bytes 65560
  51.4 3.1 %finish.1 = (f32[32,128,128]{2,1,0:T(8,128)}, f32[128,128]{1,0:T(8,128)}) custom-call(bf16[32,128,256]{2,1,0:T(8,128)(2,1)S(1)} %copy-done, f32[128,128]{1,0:T(8,128)S(1)} %copy-done.1, f32[128,128]{1,0:T(8,128)S(1)} %copy-done.2), custom_call_target="tpu_custom_call" | custom-call | tf_op jit(solution)/shard_map/finish/pallas_call | solution.py:523
Async XLA Ops:
  48.2 1.6 %copy-start = (bf16[32,128,256]{2,1,0:T(8,128)(2,1)S(1)}, bf16[32,128,256]{2,1,0:T(8,128)(2,1)}, u32[]{:S(2)}) copy-start(bf16[32,128,256]{2,1,0:T(8,128)(2,1)} %get-tuple-element.5.wide) | copy-start | bytes 6291460
  49.7 0.8 %copy-start.1 = (f32[128,128]{1,0:T(8,128)S(1)}, f32[128,128]{1,0:T(8,128)}, u32[]{:S(2)}) copy-start(f32[128,128]{1,0:T(8,128)} %get-tuple-element.6.inv) | copy-start | bytes 196612
  50.6 0.8 %copy-start.2 = (f32[128,128]{1,0:T(8,128)S(1)}, f32[128,128]{1,0:T(8,128)}, u32[]{:S(2)}) copy-start(f32[128,128]{1,0:T(8,128)} %get-tuple-element.7.proj) | copy-start | bytes 196612

commit v2 on v1

--- a/solution.py
+++ b/solution.py
@@ -17,6 +17,17 @@
     hi = x.astype(BF)
     lo = (x - hi.astype(F32)).astype(BF)
     return hi, lo
+
+
+def dot_halves(a, b):
+    b_both = jnp.concatenate(split2(b), axis=1)
+    both = jnp.dot(
+        jnp.concatenate(split2(a), axis=1),
+        jnp.concatenate([b_both, b_both], axis=0),
+        preferred_element_type=F32,
+    )
+    half = b.shape[1]
+    return both[:, :half] + both[:, half:]
 
 
 def split3(x):
@@ -412,10 +423,11 @@
             aug[base + 8 :, :] = aug[base + 8 :, :] - update[base + 8 :, :]
 
     blocks = width // 8
-    for b in range(blocks // 2):
+    early = 3 * blocks // 8
+    for b in range(early):
         chol_block(b)
     rs_finish(1)
-    for b in range(blocks // 2, blocks):
+    for b in range(early, blocks):
         chol_block(b)
     ag_finish(1)
 
@@ -444,19 +456,10 @@
     )
     basis[...] = (both[:, :width] + both[:, width:]).reshape(count, orb, width)
 
-    @pl.when(pl.program_id(0) == 0)
+    @pl.when(pl.program_id(0) == jnp.minimum(1, pl.num_programs(0) - 1))
     def _():
-        highest = lax.Precision.HIGHEST
-        right = jnp.dot(
-            inverse, proj[...], precision=highest, preferred_element_type=F32
-        )
-        reduced[...] = lax.dot_general(
-            right,
-            inverse,
-            (((1,), (1,)), ((), ())),
-            precision=highest,
-            preferred_element_type=F32,
-        )
+        right = dot_halves(inverse, proj[...])
+        reduced[...] = dot_halves(right, inverse.T)
 
 
 def local(states, onsite_blocks, hop_blocks, onsite_index, hop_index):
@@ -518,7 +521,7 @@
     )(hop_index.T, onsite_index, states, onsite_blocks, hop_blocks)
     total = cells * n
     factor = float(total * orb) ** 0.5
-    count = max(d for d in range(1, 9) if cells % d == 0)
+    count = max(d for d in range(1, 17) if cells % d == 0)
     square = pl.BlockSpec((width, width), lambda i: (0, 0))
     basis, reduced = pl.pallas_call(
         functools.partial(finish, factor),
@@ -534,7 +537,7 @@
         ],
         out_specs=(pl.BlockSpec((count, orb, width), lambda i: (i, 0, 0)), square),
         scratch_shapes=[pltpu.VMEM((2 * width, 2 * width), BF)],
-        compiler_params=pltpu.CompilerParams(vmem_limit_bytes=32 * 2**20),
+        compiler_params=pltpu.CompilerParams(vmem_limit_bytes=60 * 2**20),
         name="finish",
     )(current, inverse, projected)
     return (basis, reduced)

time: 54.8 us -> 51.2 us (0.934)
  local copies, waits for them, and re-layouts: 3.26 us -> 0 us
    unnamed x6 -> x0, local copies, waits for them, and re-layouts: 3.26 us -> none
    pallas_call x1, Pallas kernels: 47.5 us -> 46.8 us  [local(): pl.pallas_call(functools.partial(kernel, n, owners), out_shape=(jax.Shape...]
where the time goes in v2:
time: 51.2 us; the launch traced here: 51 us
  Pallas kernels  50.4 us (98%)
  between operations  0.64 us (1%)
    pallas_call x1, Pallas kernels, local(): pl.pallas_call(functools.partial(kernel, n, owners), out_shape=(jax.Shape...  46.8 us
    pallas_call x1, Pallas kernels, local(): pl.pallas_call(functools.partial(finish, factor), grid=(cells // count,),...  3.53 us

profile of v2, /device:TPU:0, one launch (start us, length us, event | category | flops | bytes accessed | tf_op | source)
XLA Modules:
  0.0 51.0 jit_solution(358646346612834098)
XLA Ops:
  0.6 46.8 %filter.1 = (bf16[32,128,256]{2,1,0:T(8,128)(2,1)}, f32[128,128]{1,0:T(8,128)}, f32[128,128]{1,0:T(8,128)}) custom-call(s32[4,32]{1,0:T(4,128)} %bitcast.1, s32[32]{0:T(128)} %on_idx.1, f32[32,128,128]{2,1,0:T(8,128)} %states_hbm.1, f32[8,128,128]{2,1,0:T(8,128)} %onsite_hbm.1, f32[16,128,128]{2,1,0:T(8,128)} %hop_hbm.1), custom_call_target="tpu_custom_call" | custom-call | tf_op jit(solution)/shard_map/filter/pallas_call | solution.py:478
  47.5 3.5 %finish.1 = (f32[32,128,128]{2,1,0:T(8,128)}, f32[128,128]{1,0:T(8,128)}) custom-call(bf16[32,128,256]{2,1,0:T(8,128)(2,1)} %get-tuple-element.5.wide, f32[128,128]{1,0:T(8,128)} %get-tuple-element.6.inv, f32[128,128]{1,0:T(8,128)} %get-tuple-element.7.proj), custom_call_target="tpu_custom_call" | custom-call | tf_op jit(solution)/shard_map/finish/pallas_call | solution.py:526

commit v3 on v2

--- a/solution.py
+++ b/solution.py
@@ -230,7 +230,7 @@
         halo_start(k + 1, out)
 
         inner = cells - 4
-        group = max(d for d in range(1, 15) if inner % d == 0)
+        group = max(d for d in range(1, 29) if inner % d == 0)
 
         @pl.loop(2, cells - 2, step=group)
         def _(c):
@@ -334,7 +334,7 @@
                     device_id_type=MESH,
                 ).wait_recv()
 
-    batch = max(d for d in range(1, 9) if cells % (2 * d) == 0)
+    batch = max(d for d in range(1, 17) if cells % (2 * d) == 0)
     gacc[...] = jnp.zeros_like(gacc)
 
     @pl.loop(0, cells, step=batch)

time: 51.2 us -> 50.8 us (level)
  no operation moved by 1% of the time
where the time goes in v3:
time: 50.8 us; the launch traced here: 50.6 us
  Pallas kernels  49.9 us (98%)
  between operations  0.64 us (1%)
    pallas_call x1, Pallas kernels, local(): pl.pallas_call(functools.partial(kernel, n, owners), out_shape=(jax.Shape...  46.4 us
    pallas_call x1, Pallas kernels, local(): pl.pallas_call(functools.partial(finish, factor), grid=(cells // count,),...  3.52 us

profile of v3, /device:TPU:0, one launch (start us, length us, event | category | flops | bytes accessed | tf_op | source)
XLA Modules:
  0.0 50.6 jit_solution(15489981249367386570)
XLA Ops:
  0.6 46.4 %filter.1 = (bf16[32,128,256]{2,1,0:T(8,128)(2,1)}, f32[128,128]{1,0:T(8,128)}, f32[128,128]{1,0:T(8,128)}) custom-call(s32[4,32]{1,0:T(4,128)} %bitcast.1, s32[32]{0:T(128)} %on_idx.1, f32[32,128,128]{2,1,0:T(8,128)} %states_hbm.1, f32[8,128,128]{2,1,0:T(8,128)} %onsite_hbm.1, f32[16,128,128]{2,1,0:T(8,128)} %hop_hbm.1), custom_call_target="tpu_custom_call" | custom-call | tf_op jit(solution)/shard_map/filter/pallas_call | solution.py:478
  47.0 3.5 %finish.1 = (f32[32,128,128]{2,1,0:T(8,128)}, f32[128,128]{1,0:T(8,128)}) custom-call(bf16[32,128,256]{2,1,0:T(8,128)(2,1)} %get-tuple-element.5.wide, f32[128,128]{1,0:T(8,128)} %get-tuple-element.6.inv, f32[128,128]{1,0:T(8,128)} %get-tuple-element.7.proj), custom_call_target="tpu_custom_call" | custom-call | tf_op jit(solution)/shard_map/finish/pallas_call | solution.py:526
